TPU v7x, 256 devices: a whole 4x4x8 slice. The times are simulated.
256 devices in a mesh: factor: 8 (over z_lo, core), dp: 32 (over z_hi, y, x).
Axes of the slice: x: 4, y: 4, z: 8 (z_hi: 2, z_lo: 4; z = z_hi * 4 + z_lo), core: 2. Of those that a mesh axis runs over, the one named last changes fastest.
Arguments:
- acts: bfloat16 [2, 65536, 4096], P(None, ('factor', 'dp'))
- grads_out: bfloat16 [2, 65536, 4096], P(None, ('factor', 'dp'))
- grad: bfloat16 [2, 4096, 4096], P(None, 'dp', 'factor'), may hold values from -0.59765625 to 0.59765625
- bases_a: float32 [16, 4096, 128], P('factor', 'dp'), may hold values from -0.5 to 0.5
- bases_g: float32 [16, 4096, 128], P('factor', 'dp'), may hold values from -0.5 to 0.5
- owner_slot: int32 [2], replicated, may hold values from 0 to 15, as said below
Outputs:
- update: bfloat16 [2, 4096, 4096], P(None, 'dp', 'factor')
Inputs may be any that keep to these rules, and one draw needn't show every extreme that they name: The values are distinct and one layer always uses the last slot; layer l belongs to owner group owner_slot[l] // 2 (the index along factor) and uses its slot owner_slot[l] % 2.
All inputs are finite; a program needn't handle non-finite values.
Results may differ from a plain program's by a relative error of at most 0.001.
Values may be sent and summed in bfloat16 or wider, within the bound.
A program may use at most 128 MiB of HBM per device.

v0:
```python
import jax
import jax.numpy as jnp
from jax import lax
from jax.sharding import PartitionSpec as P

BLOCK = 128
SLOTS = 2


damping = 0.05


def from_root(x, axis, root):
    mine = lax.axis_index(axis) == root
    return lax.psum(jnp.where(mine, x, jnp.zeros_like(x)), axis)


def eigen_scale(factor_blocks, basis):
    turned = jnp.einsum("nbc,ncd->nbd", factor_blocks, basis, precision=lax.Precision.HIGHEST)
    return jnp.sum(basis * turned, axis=1)


def precondition(gradient, basis_left, basis_right, scale_left, scale_right):
    left_count = basis_left.shape[0]
    right_count = basis_right.shape[0]
    values = gradient.astype(jnp.float32).reshape(left_count, BLOCK, right_count, BLOCK)
    rotated = jnp.einsum("ibc,ibjd->icjd", basis_left, values, precision=lax.Precision.HIGHEST)
    inner = jnp.einsum("icjd,jde->icje", rotated, basis_right, precision=lax.Precision.HIGHEST)
    scaled = inner / (scale_left[:, :, None, None] * scale_right[None, None, :, :] + damping)
    restored = jnp.einsum("icje,jfe->icjf", scaled, basis_right, precision=lax.Precision.HIGHEST)
    result = jnp.einsum("iac,icjf->iajf", basis_left, restored, precision=lax.Precision.HIGHEST)
    return result.reshape(left_count * BLOCK, right_count * BLOCK).astype(jnp.bfloat16)


def slot_bases(bases, owner_slot, position, local_blocks):
    local_slot = owner_slot[position] % SLOTS
    return lax.dynamic_index_in_dim(bases, local_slot, 0, keepdims=False).reshape(
        local_blocks, BLOCK, BLOCK
    )


def body(acts, grads_out, grad, bases_a, bases_g, owner_slot):
    layer_count, row_count, feature_width = acts.shape
    dp_count = lax.axis_size("dp")
    factor_count = lax.axis_size("factor")
    total_rows = row_count * dp_count * factor_count
    block_count = feature_width // BLOCK
    local_blocks = block_count // dp_count
    slab_width = grad.shape[2]
    slab_blocks = slab_width // BLOCK
    first_block = lax.axis_index("factor") * slab_blocks
    stacked = jnp.stack([acts, grads_out], axis=1)
    grouped = stacked.reshape(layer_count, 2, row_count, block_count, BLOCK)
    partial_terms = jnp.einsum(
        "lsrnb,lsrnc->lsnbc", grouped, grouped, preferred_element_type=jnp.float32
    )
    summed = lax.psum_scatter(partial_terms, "dp", scatter_dimension=2, tiled=True)
    factors = lax.psum(summed, "factor") / total_rows
    scale_list = []
    for position in range(layer_count):
        basis_left = slot_bases(bases_a, owner_slot, position, local_blocks)
        basis_right = slot_bases(bases_g, owner_slot, position, local_blocks)
        scale_list.append(
            jnp.stack(
                [
                    eigen_scale(factors[position, 0], basis_left),
                    eigen_scale(factors[position, 1], basis_right),
                ]
            )
        )
    scales = jnp.stack(scale_list)
    results = []
    for position in range(layer_count):
        owner_group = owner_slot[position] // SLOTS
        basis_left = slot_bases(bases_a, owner_slot, position, local_blocks)
        basis_right = slot_bases(bases_g, owner_slot, position, local_blocks)
        scale_left = scales[position, 0]
        scale_right = scales[position, 1]
        full_rows = lax.all_gather(grad[position], "factor", axis=1, tiled=True)
        right_all, right_scales = (
            lax.all_gather(basis_right, "dp", axis=0, tiled=True),
            lax.all_gather(scale_right, "dp", axis=0, tiled=True),
        )
        owned = precondition(full_rows, basis_left, right_all, scale_left, right_scales)
        received = from_root(owned, "factor", owner_group)
        update = lax.dynamic_slice_in_dim(received, first_block * BLOCK, slab_width, 1)
        results.append(update)
    return jnp.stack(results)


def solution(mesh):
    in_specs = (
        P(None, ("factor", "dp"), None),
        P(None, ("factor", "dp"), None),
        P(None, "dp", "factor"),
        P("factor", "dp", None),
        P("factor", "dp", None),
        P(),
    )
    out_specs = P(None, "dp", "factor")
    return jax.shard_map(body, mesh=mesh, in_specs=in_specs, out_specs=out_specs, check_vma=False)
```

profile of v0, /device:TPU:32, one launch (start us, length us, event | category | flops | bytes accessed | tf_op | source)
XLA Modules:
  0.0 1178.9 jit_solution(13569829372287974009)
XLA Ops:
  9.2 1.3 fusion.56
  13.9 1.6 constant_dynamic-slice_fusion.1
  15.6 6.3 copy.46
  21.9 6.3 copy.48
  28.2 6.3 copy.47
  34.5 6.3 copy.49
  40.9 11.6 fusion
  54.9 3.6 fusion.36
  58.5 25.2 %all-gather.15.cloned.1.call-done = bf16[1,128,4096]{1,2,0:T(8,128)(2,1)} async-done(((bf16[1,128,512]{1,2,0:T(8,128)(2,1)}), bf16[1,128,4096]{1,2,0:T(8,128)(2,1)}) %all-gather.15.cloned.1.call-update) | async-done | bytes 1048592 | tf_op jit(solution)/shard_map/all_gather | solution.py:79
  83.7 2.2 fusion.32
  86.0 94.1 %all-gather.9.cloned.1.call-done = f32[32,128,128]{2,1,0:T(8,128)} async-done(((f32[1,128,128]{2,1,0:T(8,128)}), f32[32,128,128]{2,1,0:T(8,128)}) %all-gather.9.cloned.1.call-update) | async-done | bytes 2097168 | tf_op jit(solution)/shard_map/all_gather | solution.py:81
  180.1 7.0 fusion.57
  187.2 519.1 %all-reduce.8.cloned.1.call-done = f32[2,2,32,128,128]{4,3,2,1,0:T(8,128)} async-done(((f32[2,2,32,128,128]{4,3,2,1,0:T(8,128)}), f32[2,2,32,128,128]{4,3,2,1,0:T(8,128)}) %all-reduce.8.cloned.1.call-update) | async-done | bytes 8388624
  706.3 2.4 constant_dynamic-slice_fusion.2
  708.9 86.4 %all-gather.11.cloned.1.call-done = f32[32,128,128]{2,1,0:T(8,128)} async-done(((f32[1,128,128]{2,1,0:T(8,128)}), f32[32,128,128]{2,1,0:T(8,128)}) %all-gather.11.cloned.1.call-update) | async-done | bytes 2097168 | tf_op jit(solution)/shard_map/all_gather | solution.py:81
  795.3 6.4 fusion.58
  801.7 58.5 %all-reduce.6.cloned.1.call-done = f32[2,2,1,128,128]{4,3,2,1,0:T(8,128)} async-done(((f32[2,2,1,128,128]{4,3,2,1,0:T(8,128)}), f32[2,2,1,128,128]{4,3,2,1,0:T(8,128)}) %all-reduce.6.cloned.1.call-update) | async-done | bytes 262160 | tf_op jit(solution)/shard_map/psum | solution.py:58
  862.1 113.4 %all-gather.1 = f32[32,1,1,128]{3,2,1,0:T(1,128)S(1)} all-gather(f32[1,1,1,128]{3,2,1,0:T(1,128)S(1)} %get-tuple-element.12), channel_id=3, replica_groups=mesh['factor'=8,'dp'=32] {'dp'}, dimensions={0}, use_global_device_ids=true | all-gather | bytes 16896 | tf_op jit(solution)/shard_map/all_gather | solution.py:82
  975.5 106.1 %all-gather.3 = f32[32,1,1,128]{3,2,1,0:T(1,128)S(1)} all-gather(f32[1,1,1,128]{3,2,1,0:T(1,128)S(1)} %get-tuple-element.14), channel_id=5, replica_groups=mesh['factor'=8,'dp'=32] {'dp'}, dimensions={0}, use_global_device_ids=true | all-gather | bytes 16896 | tf_op jit(solution)/shard_map/all_gather | solution.py:82
  1081.6 4.9 fusion.10
  1086.5 2.9 fusion.4
  1089.4 2.5 fusion.7
  1091.9 3.0 fusion.5
  1094.9 75.5 %all-reduce.10.cloned.1.call-done = (bf16[128,4096]{1,0:T(8,128)(2,1)}, bf16[128,4096]{1,0:T(8,128)(2,1)}) async-done(((bf16[128,4096]{1,0:T(8,128)(2,1)}, bf16[128,4096]{1,0:T(8,128)(2,1)}), (bf16[128,4096]{1,0:T(8,128)(2,1)}, bf16[128,4096]{1,0:T(8,128)(2,1)})) %all-reduce.10.cloned.1.call-update) | async-done | bytes 2097168 | tf_op jit(solution)/shard_map/psum | solution.py:15
  (42 shorter events, 7.8 us)
Async XLA Ops:
  6.5 48.4 %all-gather.13.cloned.1.call-start = ((), (), s32[]{:S(2)}) async-start(), calls=%async_computation.3 | async-start | bytes 1179648 | tf_op jit(solution)/shard_map/all_gather | solution.py:79
  8.3 75.4 %all-gather.15.cloned.1.call-start = ((), (), s32[]{:S(2)}) async-start(), calls=%async_computation.4 | async-start | bytes 1179648 | tf_op jit(solution)/shard_map/all_gather | solution.py:79
  9.1 171.0 %all-gather.9.cloned.1.call-start = ((), (), s32[]{:S(2)}) async-start(), calls=%async_computation | async-start | bytes 2162688 | tf_op jit(solution)/shard_map/all_gather | solution.py:81
  15.5 690.8 %all-reduce.8.cloned.1.call-start = ((), (), s32[]{:S(2)}) async-start(), calls=%async_computation.5 | async-start | bytes 16777216
  52.4 1.8 copy-start.5
  52.4 2.5 copy-start.2
  52.5 742.8 %all-gather.11.cloned.1.call-start = ((), (), s32[]{:S(2)}) async-start(), calls=%async_computation.2 | async-start | bytes 2162688 | tf_op jit(solution)/shard_map/all_gather | solution.py:81
  53.1 807.1 %all-reduce.6.cloned.1.call-start = ((), (), s32[]{:S(2)}) async-start(), calls=%async_computation.1 | async-start | bytes 524288 | tf_op jit(solution)/shard_map/psum | solution.py:58
  708.6 152.5 %copy-start.4 = (f32[1,128,128]{2,1,0:T(8,128)S(1)}, f32[1,128,128]{2,1,0:T(8,128)}, u32[]{:S(2)}) copy-start(f32[1,128,128]{2,1,0:T(8,128)} %get-tuple-element.9) | copy-start | bytes 196612
  708.6 153.0 %copy-start.3 = (f32[1,128,128]{2,1,0:T(8,128)S(1)}, f32[1,128,128]{2,1,0:T(8,128)}, u32[]{:S(2)}) copy-start(f32[1,128,128]{2,1,0:T(8,128)} %get-tuple-element.10) | copy-start | bytes 196612
  708.7 461.7 %all-reduce.10.cloned.1.call-start = ((), (), s32[]{:S(2)}) async-start(), calls=%async_computation.6 | async-start | bytes 4194304 | tf_op jit(solution)/shard_map/psum | solution.py:15
  1081.6 7.8 copy-start.1
  1086.5 2.9 copy-start
Sparse Core Ops, SparseCore 0:
  9.1 36.7 all-gather.12
  47.7 36.0 all-gather.14
  87.3 92.8 all-gather.8
  182.7 523.5 all-reduce.7
  709.6 85.6 all-gather.10
  797.8 62.3 all-reduce.5
  1095.0 75.3 all-reduce.9
where the time goes:
time: 1180 us
  waiting for transfers between devices  859 us (73%)
  blocking collectives  219 us (19%)
  matrix products  45 us (4%)
  local copies, waits for them, and re-layouts  34.7 us (3%)
  between operations  18.2 us (2%)
    unnamed x8, waiting for transfers between devices  520 us
    all_gather x2, blocking collectives, body(): lax.all_gather(scale_right, 'dp', axis=0, tiled=True)  219 us
    all_gather x2, waiting for transfers between devices, body(): lax.all_gather(basis_right, 'dp', axis=0, tiled=True)  181 us
    psum x1, waiting for transfers between devices, from_root(): return lax.psum(jnp.where(mine, x, jnp.zeros_like(x)), axis)  75.5 us
    psum x1, waiting for transfers between devices, body(): factors = lax.psum(summed, 'factor') / total_rows  58.5 us
    all_gather x2, waiting for transfers between devices, body(): full_rows = lax.all_gather(grad[position], 'factor', axis=1, tiled=True)  25.2 us
  transfers between devices with their start and end apart: 7, of which 6 were waited for; matrix products, arithmetic and copies ran while one was open for 5% of the time, Pallas kernels for 0%

commit v1 on v0

v1 whole, which is shorter than its diff:
```python
import functools

import jax
import jax.numpy as jnp
from jax import lax
from jax.experimental import pallas as pl
from jax.experimental.pallas import tpu as pltpu
from jax.sharding import PartitionSpec as P

MESH = pl.DeviceIdType.MESH
B = 128
SLOTS = 2
DAMPING = 0.05
HIGHEST = lax.Precision.HIGHEST
F32 = jnp.float32

CHUNK = 8 * B + 8
PIECE = 2 * B + 8
ORDER = (2, 1, 3, 0)


def dot(a, b, ca, cb, precision=None):
    return lax.dot_general(a, b, (((ca,), (cb,)), ((), ())), precision=precision, preferred_element_type=F32)


def kernel(total_rows, slot_ref, acts, grads, grad, bases_a, bases_g, out,
           xs, gs, bs, part, core_in, own, in1, two, in2, qc, qc_in, qs, qs_in, qm, qbuf, qa, qg,
           zs, zr, sa, sg, keep, inner_s,
           ld, s_core, r_core, s_one, r_one, s_two, r_two, s_q, r_q, s_rs, r_rs, s_ag, r_ag,
           s_qy, r_qy, s_qx, r_qx, s_z, r_z, s_xy, r_xy, s_p, r_p):
    f = lax.axis_index("factor")
    d = lax.axis_index("dp")
    z_lo, c = f // 2, f % 2
    z_hi, y, x = d // 16, (d // 4) % 4, d % 4
    z = 4 * z_hi + z_lo
    row_col = 4 * y + x
    other = 1 - c
    first, second = x + c * (y - x), y + c * (x - y)
    first_other = x + other * (y - x)
    side = 1 - (y + c) % 2
    source_row = 2 * (z_lo % 2) + c
    is_source = y == source_row
    half_here = z_lo // 2

    def at(zz, yy, xx, cc):
        return (2 * (zz % 4) + cc, 16 * (zz // 4) + 4 * yy + xx)

    def ring(t, u):
        return at(z, u + c * (t - u), t + c * (u - t), c)

    def remote(src, dst, send, recv, to):
        return pltpu.make_async_remote_copy(src_ref=src, dst_ref=dst, send_sem=send, recv_sem=recv,
                                            device_id=to, device_id_type=MESH)

    partner = at(z, y, x, other)

    loads = [
        pltpu.make_async_copy(bases_a, bs.at[0], ld.at[0]),
        pltpu.make_async_copy(bases_g, bs.at[1], ld.at[1]),
        pltpu.make_async_copy(acts, xs.at[0], ld.at[2]),
        pltpu.make_async_copy(grads, xs.at[1], ld.at[3]),
        pltpu.make_async_copy(grad, gs, ld.at[4]),
    ]
    for copy in loads:
        copy.start()

    barrier = pltpu.get_barrier_semaphore()

    def signal(to):
        pl.semaphore_signal(barrier, inc=1, device_id=to, device_id_type=MESH)

    signal(partner)
    for k in range(1, 16):
        n = (row_col + k) % 16
        signal(at(z, n // 4, n % 4, c))
    for k in range(1, 8):
        signal(at((z + k) % 8, y, x, c))

    loads[0].wait()
    loads[1].wait()
    for l in range(2):
        slot = slot_ref[l]
        mine = (slot // SLOTS) == f
        for which, sd in ((0, side), (1, 1 - side)):
            picked = jnp.where(slot % SLOTS == 0, bs[sd, 0], bs[sd, 1])
            qc[which, l] = jnp.where(mine, picked, jnp.zeros_like(picked))
    pl.semaphore_wait(barrier, 23)

    core_q = remote(qc.at[1], qc_in, s_q, r_q, partner)
    core_q.start()

    iota_r = lax.broadcasted_iota(jnp.int32, (B, B), 0)
    iota_c = lax.broadcasted_iota(jnp.int32, (B, B), 1)
    upper = iota_r <= iota_c
    on_diag = iota_r == iota_c

    def chunk_terms(core, t, dst, add):
        def one(m, carry):
            u, h = m // 2, m % 2
            xb, yb = t + core * (u - t), u + core * (t - u)
            col = pl.multiple_of((16 * h + 4 * yb + xb) * B, B)
            sd = 1 - (yb + core) % 2
            x0 = xs[sd, 0, :, pl.ds(col, B)]
            x1 = xs[sd, 1, :, pl.ds(col, B)]
            f0 = dot(x0, x0, 0, 0)
            f1 = dot(x1, x1, 0, 0)
            packed = jnp.where(upper, f0, f1)
            diag = jnp.sum(jnp.where(on_diag, f1, 0.0), axis=0, keepdims=True)
            rows = pl.ds(pl.multiple_of(m * B, B), B)
            row = pl.ds(8 * B + m, 1)
            if add is not None:
                packed = packed + add[rows, :]
                diag = diag + add[row, :]
            dst[rows, :] = packed
            dst[row, :] = diag
            return carry

        lax.fori_loop(0, 8, one, 0)

    loads[2].wait()
    loads[3].wait()

    core_copies, one_copies = [], []

    def for_partner(k):
        chunk_terms(other, (first_other + ORDER[k]) % 4, part.at[k], None)
        copy = remote(part.at[k], core_in.at[k], s_core.at[k], r_core.at[k], partner)
        copy.start()
        core_copies.append(copy)

    def for_ring(k):
        core_copies[k].wait_recv()
        t = (first + ORDER[k]) % 4
        chunk_terms(c, t, own.at[k], core_in.at[k])
        if k < 3:
            copy = remote(own.at[k], in1.at[k], s_one.at[k], r_one.at[k], ring(t, second))
            copy.start()
            one_copies.append(copy)

    for_partner(0)

    core_q.wait_recv()
    for l in range(2):
        qs[l] = qc[0, l] + qc_in[l]
    rs_copies = []
    for k in range(1, 4):
        zz = (z_lo + k) % 4
        copy = remote(qs.at[:, pl.ds(pl.multiple_of(32 * zz, 32), 32), :], qs_in.at[k - 1],
                      s_rs.at[k - 1], r_rs.at[k - 1], at(4 * z_hi + zz, y, x, c))
        copy.start()
        rs_copies.append(copy)

    for_partner(1)
    for_ring(0)

    for copy in rs_copies:
        copy.wait_recv()
    here = pl.ds(pl.multiple_of(32 * z_lo, 32), 32)
    summed = qs[:, here, :] + qs_in[0] + qs_in[1] + qs_in[2]
    qm[...] = summed
    qbuf[z_hi, :, here, :] = summed
    ag_copies = []
    for k in range(1, 8):
        copy = remote(qm, qbuf.at[z_hi, :, here, :], s_ag.at[k - 1], r_ag.at[k - 1], at((z + k) % 8, y, x, c))
        copy.start()
        ag_copies.append(copy)

    for_partner(2)
    for_ring(1)
    for_partner(3)
    for_ring(2)
    for_ring(3)

    for k in range(1, 8):
        zz = (z + 8 - k) % 8
        rows = pl.ds(pl.multiple_of(32 * (zz % 4), 32), 32)
        remote(qm, qbuf.at[zz // 4, :, rows, :], s_ag.at[k - 1], r_ag.at[k - 1], partner).wait_recv()

    qy_copies = []
    for k in range(1, 4):
        copy = remote(qbuf.at[half_here], qg.at[x], s_qy.at[k - 1], r_qy, at(z, (y + k) % 4, x, c))
        qy_copies.append(copy)
    qa_copy = remote(qbuf.at[z_hi], qa, s_p.at[0], r_p.at[0], partner)

    @pl.when(is_source)
    def _():
        for copy in qy_copies:
            copy.start()
        qg[x] = qbuf[half_here]

    @pl.when(side == 0)
    def _():
        qa_copy.start()
        qa[...] = qbuf[z_hi]

    for copy in one_copies:
        copy.wait_recv()
    diags = slice(8 * B, CHUNK)
    diag_sum = own[3, diags, :] + in1[0, diags, :] + in1[1, diags, :] + in1[2, diags, :]
    two_copies = []
    for k in range(4):
        u = (second + ORDER[k]) % 4
        rows = pl.ds(pl.multiple_of(2 * B * u, 2 * B), 2 * B)
        two[k, : 2 * B, :] = own[3, rows, :] + in1[0, rows, :] + in1[1, rows, :] + in1[2, rows, :]
        two[k, 2 * B :, :] = diag_sum
        if k < 3:
            copy = remote(two.at[k], in2.at[k], s_two.at[k], r_two.at[k], ring(first, u))
            copy.start()
            two_copies.append(copy)

    @pl.when(jnp.logical_not(is_source))
    def _():
        qy_copies[0].wait_recv()

    qx_copies = []
    for k in range(1, 4):
        copy = remote(qg.at[x], qg.at[x], s_qx.at[k - 1], r_qx.at[k - 1], at(z, y, (x + k) % 4, c))
        copy.start()
        qx_copies.append(copy)

    for copy in two_copies:
        copy.wait_recv()

    zs[...] = jnp.zeros_like(zs)
    for h in range(2):
        rows = slice(h * B, (h + 1) * B)
        packed = two[3, rows, :] + in2[0, rows, :] + in2[1, rows, :] + in2[2, rows, :]
        row = pl.ds(2 * B + 2 * second + h, 1)
        diag = two[3, row, :] + in2[0, row, :] + in2[1, row, :] + in2[2, row, :]
        m0 = jnp.where(upper, jnp.where(on_diag, packed, 2.0 * packed), 0.0)
        m1 = jnp.where(upper, jnp.where(on_diag, jnp.broadcast_to(diag, (B, B)), 0.0), 2.0 * packed)
        for l, m in ((0, m0), (1, m1)):
            q = qbuf[h, l]
            zs[2 * h + l : 2 * h + l + 1, :] = jnp.sum(q * dot(m, q, 1, 0, HIGHEST), axis=0, keepdims=True)
    z_copies = []
    for k in range(1, 8):
        copy = remote(zs, zr.at[k], s_z.at[k - 1], r_z.at[k - 1], at((z + k) % 8, y, x, c))
        copy.start()
        z_copies.append(copy)
    zr[0] = zs[...]

    @pl.when(side == 1)
    def _():
        qa_copy.wait_recv()

    for k in range(1, 4):
        from_x = (x + 4 - k) % 4
        remote(qg.at[x], qg.at[from_x], s_qx.at[k - 1], r_qx.at[k - 1], partner).wait_recv()
    loads[4].wait()
    for l in range(2):
        rotated = dot(qa[l], gs[l].astype(F32), 0, 0, HIGHEST)
        for q in range(4):
            inner_s[l, :, q * B : (q + 1) * B] = dot(rotated[:, q * B : (q + 1) * B], qg[q, l], 1, 0, HIGHEST)

    for copy in z_copies:
        copy.wait_recv()
    scales = zr[0]
    for k in range(1, 8):
        scales = scales + zr[k]
    scales = scales / total_rows
    keep[...] = scales

    xy_copies = []
    for k in range(1, 16):
        n = (row_col + k) % 16
        xy_copies.append(remote(zs, sg.at[x], s_xy.at[k - 1], r_xy.at[x], at(z, n // 4, n % 4, c)))
    sa_copy = remote(zs, sa, s_p.at[1], r_p.at[1], partner)

    for copy in z_copies:
        copy.wait_send()

    @pl.when(is_source)
    def _():
        zs[:2, :] = keep[pl.ds(2 * half_here, 2), :]
        for copy in xy_copies:
            copy.start()
        sg[x] = zs[...]

    @pl.when(side == 0)
    def _():
        zs[:2, :] = keep[pl.ds(2 * z_hi, 2), :]
        sa_copy.start()
        sa[...] = zs[...]

    @pl.when(side == 1)
    def _():
        sa_copy.wait_recv()

    for q in range(4):
        @pl.when(jnp.logical_not(jnp.logical_and(is_source, x == q)))
        def _():
            remote(zs, sg.at[q], s_xy.at[0], r_xy.at[q], partner).wait_recv()

    for l in range(2):
        left = jnp.transpose(jnp.broadcast_to(sa[l : l + 1, :], (B, B)))
        for q in range(4):
            cols = slice(q * B, (q + 1) * B)
            scaled = inner_s[l, :, cols] / (left * sg[q, l : l + 1, :] + DAMPING)
            inner_s[l, :, cols] = dot(scaled, qg[q, l], 1, 1, HIGHEST)
        out[l] = dot(qa[l], inner_s[l], 1, 0, HIGHEST).astype(out.dtype)

    for copy in [core_q] + core_copies + one_copies + rs_copies + ag_copies + two_copies + qx_copies:
        copy.wait_send()

    @pl.when(is_source)
    def _():
        for copy in qy_copies + xy_copies:
            copy.wait_send()

    @pl.when(side == 0)
    def _():
        qa_copy.wait_send()
        sa_copy.wait_send()


def body(acts, grads_out, grad, bases_a, bases_g, owner_slot):
    rows = acts.shape[1]
    total_rows = rows * lax.axis_size("dp") * lax.axis_size("factor")
    dma = pltpu.SemaphoreType.DMA
    scratch = [
        pltpu.VMEM((2,) + acts.shape, acts.dtype),
        pltpu.VMEM(grad.shape, grad.dtype),
        pltpu.VMEM((2,) + bases_a.shape, F32),
        pltpu.VMEM((4, CHUNK, B), F32),
        pltpu.VMEM((4, CHUNK, B), F32),
        pltpu.VMEM((4, CHUNK, B), F32),
        pltpu.VMEM((3, CHUNK, B), F32),
        pltpu.VMEM((4, PIECE, B), F32),
        pltpu.VMEM((3, PIECE, B), F32),
        pltpu.VMEM((2, 2, B, B), F32),
        pltpu.VMEM((2, B, B), F32),
        pltpu.VMEM((2, B, B), F32),
        pltpu.VMEM((3, 2, 32, B), F32),
        pltpu.VMEM((2, 32, B), F32),
        pltpu.VMEM((2, 2, B, B), F32),
        pltpu.VMEM((2, B, B), F32),
        pltpu.VMEM((4, 2, B, B), F32),
        pltpu.VMEM((8, B), F32),
        pltpu.VMEM((8, 8, B), F32),
        pltpu.VMEM((8, B), F32),
        pltpu.VMEM((4, 8, B), F32),
        pltpu.VMEM((8, B), F32),
        pltpu.VMEM((2, B, 4 * B), F32),
        dma((5,)),
        dma((4,)), dma((4,)),
        dma((3,)), dma((3,)),
        dma((3,)), dma((3,)),
        dma, dma,
        dma((3,)), dma((3,)),
        dma((7,)), dma((7,)),
        dma((3,)), dma,
        dma((3,)), dma((3,)),
        dma((7,)), dma((7,)),
        dma((15,)), dma((4,)),
        dma((2,)), dma((2,)),
    ]
    hbm = pl.BlockSpec(memory_space=pl.ANY)
    return pl.pallas_call(
        functools.partial(kernel, total_rows),
        out_shape=jax.ShapeDtypeStruct(grad.shape, jnp.bfloat16),
        in_specs=[pl.BlockSpec(memory_space=pltpu.SMEM)] + [hbm] * 5,
        out_specs=pl.BlockSpec(memory_space=pltpu.VMEM),
        scratch_shapes=scratch,
        compiler_params=pltpu.CompilerParams(
            collective_id=0, has_side_effects=True, vmem_limit_bytes=48 * 1024 * 1024
        ),
        cost_estimate=pl.CostEstimate(flops=2 * 10**9, bytes_accessed=10**7, transcendentals=0),
    )(owner_slot, acts, grads_out, grad, bases_a, bases_g)


def solution(mesh):
    tokens = P(None, ("factor", "dp"), None)
    bases = P("factor", "dp", None)
    split = P(None, "dp", "factor")
    in_specs = (tokens, tokens, split, bases, bases, P())
    return jax.shard_map(body, mesh=mesh, in_specs=in_specs, out_specs=split, check_vma=False)
```

time: 1180 us -> 59.6 us (0.05)
  the two profiles are of different devices: /device:TPU:32 before, /device:TPU:33 now
where the time goes in v1:
time: 59.6 us; the launch traced here: 59.4 us
  Pallas kernels  53.1 us (89%)
  local copies, waits for them, and re-layouts  6.3 us (11%)
    pallas_call x1, Pallas kernels, body(): pl.pallas_call(functools.partial(kernel, total_rows), out_shape=jax.Shape...  53.1 us
    unnamed x11, local copies, waits for them, and re-layouts  6.3 us

profile of v1, /device:TPU:33, one launch (start us, length us, event | category | flops | bytes accessed | tf_op | source)
XLA Modules:
  0.0 59.4 jit_solution(8874653632375497673)
XLA Ops:
  0.0 0.0 copy-start
  0.0 2.2 %copy-done = bf16[2,256,4096]{2,1,0:T(8,128)(2,1)S(1)} copy-done((bf16[2,256,4096]{2,1,0:T(8,128)(2,1)S(1)}, bf16[2,256,4096]{2,1,0:T(8,128)(2,1)}, u32[]{:S(2)}) %copy-start) | copy-done | bytes 4194328
  2.2 0.0 copy-start.1
  2.2 0.9 %copy-done.1 = bf16[2,128,512]{2,1,0:T(8,128)(2,1)S(1)} copy-done((bf16[2,128,512]{2,1,0:T(8,128)(2,1)S(1)}, bf16[2,128,512]{2,1,0:T(8,128)(2,1)}, u32[]{:S(2)}) %copy-start.1) | copy-done | bytes 262168
  3.1 0.0 copy-start.2
  3.1 0.9 %copy-done.2 = f32[2,128,128]{2,1,0:T(8,128)S(1)} copy-done((f32[2,128,128]{2,1,0:T(8,128)S(1)}, f32[2,128,128]{2,1,0:T(8,128)}, u32[]{:S(2)}) %copy-start.2) | copy-done | bytes 131096
  4.0 0.0 copy-start.3
  4.0 0.9 %copy-done.3 = f32[2,128,128]{2,1,0:T(8,128)S(1)} copy-done((f32[2,128,128]{2,1,0:T(8,128)S(1)}, f32[2,128,128]{2,1,0:T(8,128)}, u32[]{:S(2)}) %copy-start.3) | copy-done | bytes 131096
  4.9 0.0 copy-start.4
  5.0 0.7 %copy-done.4 = s32[2]{0:T(128)S(1)} copy-done((s32[2]{0:T(128)S(1)}, s32[2]{0:T(128)}, u32[]{:S(2)}) %copy-start.4) | copy-done | bytes 32
  5.6 53.1 %shard_map.64 = bf16[2,128,512]{2,1,0:T(8,128)(2,1)S(1)} custom-call(s32[2]{0:T(128)S(1)} %copy-done.4, bf16[2,256,4096]{2,1,0:T(8,128)(2,1)S(1)} %copy-done, bf16[2,256,4096]{2,1,0:T(8,128)(2,1)} %grads.1, bf16[2,128,512]{2,1,0:T(8,128)(2,1)S(1)} %copy-done.1, f32[2,128,128]{2,1,0:T(8,128)S(1)} %copy-done.2, f32[2,128,128]{2,1,0:T(8,128)S(1)} %copy-done.3), custom_call_target="tpu_custom_call" | custom-call | flops 2000000000 | bytes 10000000 | tf_op jit(solution)/shard_map/pallas_call | solution.py:358
  58.7 0.7 %copy.8 = bf16[2,128,512]{2,1,0:T(8,128)(2,1)} copy(bf16[2,128,512]{2,1,0:T(8,128)(2,1)S(1)} %shard_map.64) | data formatting | bytes 524288
Async XLA Ops:
  0.0 2.2 %copy-start = (bf16[2,256,4096]{2,1,0:T(8,128)(2,1)S(1)}, bf16[2,256,4096]{2,1,0:T(8,128)(2,1)}, u32[]{:S(2)}) copy-start(bf16[2,256,4096]{2,1,0:T(8,128)(2,1)} %acts.1) | copy-start | bytes 12582916
  2.2 0.9 %copy-start.1 = (bf16[2,128,512]{2,1,0:T(8,128)(2,1)S(1)}, bf16[2,128,512]{2,1,0:T(8,128)(2,1)}, u32[]{:S(2)}) copy-start(bf16[2,128,512]{2,1,0:T(8,128)(2,1)} %grad.1) | copy-start | bytes 786436
  3.1 0.9 %copy-start.2 = (f32[2,128,128]{2,1,0:T(8,128)S(1)}, f32[2,128,128]{2,1,0:T(8,128)}, u32[]{:S(2)}) copy-start(f32[2,128,128]{2,1,0:T(8,128)} %bases_a.1) | copy-start | bytes 393220
  4.0 0.9 %copy-start.3 = (f32[2,128,128]{2,1,0:T(8,128)S(1)}, f32[2,128,128]{2,1,0:T(8,128)}, u32[]{:S(2)}) copy-start(f32[2,128,128]{2,1,0:T(8,128)} %bases_g.1) | copy-start | bytes 393220
  4.9 0.7 %copy-start.4 = (s32[2]{0:T(128)S(1)}, s32[2]{0:T(128)}, u32[]{:S(2)}) copy-start(s32[2]{0:T(128)} %slot_ref.1) | copy-start | bytes 28

commit v2 on v1

--- a/solution.py
+++ b/solution.py
@@ -16,6 +16,9 @@
 
 CHUNK = 8 * B + 8
 PIECE = 2 * B + 8
+SIDE = 24
+FULL = 32500.0
+TINY = 1e-37
 ORDER = (2, 1, 3, 0)
 
 
@@ -24,9 +27,9 @@
 
 
 def kernel(total_rows, slot_ref, acts, grads, grad, bases_a, bases_g, out,
-           xs, gs, bs, part, core_in, own, in1, two, in2, qc, qc_in, qs, qs_in, qm, qbuf, qa, qg,
-           zs, zr, sa, sg, keep, inner_s,
-           ld, s_core, r_core, s_one, r_one, s_two, r_two, s_q, r_q, s_rs, r_rs, s_ag, r_ag,
+           xs, gs, bs, part, core_in, own, code, norm, in_code, in_norm, two, in2, qc, qc_in, qs, qs_in, qm, qbuf, qa, qg,
+           zs, zr, sa, sg, keep, rot, inner_s,
+           ld, s_core, r_core, s_one, r_one, s_norm, r_norm, s_two, r_two, s_q, r_q, s_rs, r_rs, s_ag, r_ag,
            s_qy, r_qy, s_qx, r_qx, s_z, r_z, s_xy, r_xy, s_p, r_p):
     f = lax.axis_index("factor")
     d = lax.axis_index("dp")
@@ -93,6 +96,28 @@
     iota_c = lax.broadcasted_iota(jnp.int32, (B, B), 1)
     upper = iota_r <= iota_c
     on_diag = iota_r == iota_c
+
+    iota_16 = lax.broadcasted_iota(jnp.int32, (16, B), 0)
+
+    def norms_of(tile, m):
+        def outer(row):
+            return dot(jnp.where(iota_16 == row, tile, 0.0).astype(jnp.bfloat16), tile.astype(jnp.bfloat16), 0, 0)
+
+        return jnp.where(upper, outer(m), outer(8 + m))
+
+    def encode(k):
+        diag0 = [jnp.sum(jnp.where(on_diag, own[k, m * B : (m + 1) * B, :], 0.0), axis=0, keepdims=True)
+                 for m in range(8)]
+        diag1 = own[k, 8 * B :, :]
+        diag = jnp.concatenate(diag0 + [diag1], axis=0)
+        inverse = jnp.where(diag > TINY, lax.rsqrt(jnp.maximum(diag, TINY)), 1.0)
+        tile = inverse.astype(jnp.bfloat16).astype(F32)
+        norm[k, :16, :] = tile
+        norm[k, 16:, :] = diag1
+        for m in range(8):
+            rows = slice(m * B, (m + 1) * B)
+            unit = own[k, rows, :] * norms_of(tile, m)
+            code[k, rows, :] = jnp.round(unit * FULL).astype(jnp.int32).astype(jnp.int16)
 
     def chunk_terms(core, t, dst, add):
         def one(m, carry):
@@ -115,10 +140,7 @@
             dst[row, :] = diag
             return carry
 
-        lax.fori_loop(0, 8, one, 0)
-
-    loads[2].wait()
-    loads[3].wait()
+        lax.fori_loop(0, 8, one, 0, unroll=True)
 
     core_copies, one_copies = [], []
 
@@ -133,11 +155,12 @@
         t = (first + ORDER[k]) % 4
         chunk_terms(c, t, own.at[k], core_in.at[k])
         if k < 3:
-            copy = remote(own.at[k], in1.at[k], s_one.at[k], r_one.at[k], ring(t, second))
-            copy.start()
-            one_copies.append(copy)
-
-    for_partner(0)
+            encode(k)
+            to = ring(t, second)
+            for copy in (remote(norm.at[k], in_norm.at[k], s_norm.at[k], r_norm.at[k], to),
+                         remote(code.at[k], in_code.at[k], s_one.at[k], r_one.at[k], to)):
+                copy.start()
+                one_copies.append(copy)
 
     core_q.wait_recv()
     for l in range(2):
@@ -150,8 +173,12 @@
         copy.start()
         rs_copies.append(copy)
 
-    for_partner(1)
+    loads[2].wait()
+    loads[3].wait()
+    for k in range(4):
+        for_partner(k)
     for_ring(0)
+    for_ring(1)
 
     for copy in rs_copies:
         copy.wait_recv()
@@ -165,9 +192,6 @@
         copy.start()
         ag_copies.append(copy)
 
-    for_partner(2)
-    for_ring(1)
-    for_partner(3)
     for_ring(2)
     for_ring(3)
 
@@ -195,13 +219,19 @@
 
     for copy in one_copies:
         copy.wait_recv()
-    diags = slice(8 * B, CHUNK)
-    diag_sum = own[3, diags, :] + in1[0, diags, :] + in1[1, diags, :] + in1[2, diags, :]
+    diag_sum = own[3, 8 * B :, :] + in_norm[0, 16:, :] + in_norm[1, 16:, :] + in_norm[2, 16:, :]
+    tiles = [in_norm[i, :16, :] for i in range(3)]
     two_copies = []
     for k in range(4):
         u = (second + ORDER[k]) % 4
-        rows = pl.ds(pl.multiple_of(2 * B * u, 2 * B), 2 * B)
-        two[k, : 2 * B, :] = own[3, rows, :] + in1[0, rows, :] + in1[1, rows, :] + in1[2, rows, :]
+        for h in range(2):
+            m = 2 * u + h
+            rows = pl.ds(pl.multiple_of(B * m, B), B)
+            total = own[3, rows, :]
+            for i in range(3):
+                unit = in_code[i, rows, :].astype(jnp.int32).astype(F32) * (1.0 / FULL)
+                total = total + unit / norms_of(tiles[i], m)
+            two[k, h * B : (h + 1) * B, :] = total
         two[k, 2 * B :, :] = diag_sum
         if k < 3:
             copy = remote(two.at[k], in2.at[k], s_two.at[k], r_two.at[k], ring(first, u))
@@ -243,14 +273,9 @@
     def _():
         qa_copy.wait_recv()
 
-    for k in range(1, 4):
-        from_x = (x + 4 - k) % 4
-        remote(qg.at[x], qg.at[from_x], s_qx.at[k - 1], r_qx.at[k - 1], partner).wait_recv()
     loads[4].wait()
     for l in range(2):
-        rotated = dot(qa[l], gs[l].astype(F32), 0, 0, HIGHEST)
-        for q in range(4):
-            inner_s[l, :, q * B : (q + 1) * B] = dot(rotated[:, q * B : (q + 1) * B], qg[q, l], 1, 0, HIGHEST)
+        rot[l] = dot(qa[l], gs[l].astype(F32), 0, 0, HIGHEST)
 
     for copy in z_copies:
         copy.wait_recv()
@@ -285,6 +310,14 @@
     @pl.when(side == 1)
     def _():
         sa_copy.wait_recv()
+
+    for k in range(1, 4):
+        from_x = (x + 4 - k) % 4
+        remote(qg.at[x], qg.at[from_x], s_qx.at[k - 1], r_qx.at[k - 1], partner).wait_recv()
+    for l in range(2):
+        for q in range(4):
+            cols = slice(q * B, (q + 1) * B)
+            inner_s[l, :, cols] = dot(rot[l, :, cols], qg[q, l], 1, 0, HIGHEST)
 
     for q in range(4):
         @pl.when(jnp.logical_not(jnp.logical_and(is_source, x == q)))
@@ -324,7 +357,10 @@
         pltpu.VMEM((4, CHUNK, B), F32),
         pltpu.VMEM((4, CHUNK, B), F32),
         pltpu.VMEM((4, CHUNK, B), F32),
-        pltpu.VMEM((3, CHUNK, B), F32),
+        pltpu.VMEM((3, 8 * B, B), jnp.int16),
+        pltpu.VMEM((3, SIDE, B), F32),
+        pltpu.VMEM((3, 8 * B, B), jnp.int16),
+        pltpu.VMEM((3, SIDE, B), F32),
         pltpu.VMEM((4, PIECE, B), F32),
         pltpu.VMEM((3, PIECE, B), F32),
         pltpu.VMEM((2, 2, B, B), F32),
@@ -341,8 +377,10 @@
         pltpu.VMEM((4, 8, B), F32),
         pltpu.VMEM((8, B), F32),
         pltpu.VMEM((2, B, 4 * B), F32),
+        pltpu.VMEM((2, B, 4 * B), F32),
         dma((5,)),
         dma((4,)), dma((4,)),
+        dma((3,)), dma((3,)),
         dma((3,)), dma((3,)),
         dma((3,)), dma((3,)),
         dma, dma,
@@ -354,7 +392,7 @@
         dma((15,)), dma((4,)),
         dma((2,)), dma((2,)),
     ]
-    hbm = pl.BlockSpec(memory_space=pl.ANY)
+    hbm = pl.BlockSpec(memory_space=pltpu.HBM)
     return pl.pallas_call(
         functools.partial(kernel, total_rows),
         out_shape=jax.ShapeDtypeStruct(grad.shape, jnp.bfloat16),
@@ -362,7 +400,7 @@
         out_specs=pl.BlockSpec(memory_space=pltpu.VMEM),
         scratch_shapes=scratch,
         compiler_params=pltpu.CompilerParams(
-            collective_id=0, has_side_effects=True, vmem_limit_bytes=48 * 1024 * 1024
+            collective_id=0, has_side_effects=True, vmem_limit_bytes=63 * 1024 * 1024
         ),
         cost_estimate=pl.CostEstimate(flops=2 * 10**9, bytes_accessed=10**7, transcendentals=0),
     )(owner_slot, acts, grads_out, grad, bases_a, bases_g)

time: 59.6 us -> 46.6 us (0.78)
  the two profiles are of different devices: /device:TPU:33 before, /device:TPU:32 now
where the time goes in v2:
time: 46.6 us; the launch traced here: 46.5 us
  Pallas kernels  44.8 us (96%)
  local copies, waits for them, and re-layouts  1.67 us (4%)
    pallas_call x1, Pallas kernels, body(): pl.pallas_call(functools.partial(kernel, total_rows), out_shape=jax.Shape...  44.8 us
    unnamed x1, local copies, waits for them, and re-layouts  1.67 us

profile of v2, /device:TPU:32, one launch (start us, length us, event | category | flops | bytes accessed | tf_op | source)
XLA Modules:
  0.0 46.5 jit_solution(15408726463897056644)
XLA Ops:
  0.0 44.8 %shard_map.64 = bf16[2,128,512]{2,1,0:T(8,128)(2,1)} custom-call(s32[2]{0:T(128)} %slot_ref.1, bf16[2,256,4096]{2,1,0:T(8,128)(2,1)} %acts.1, bf16[2,256,4096]{2,1,0:T(8,128)(2,1)} %grads.1, bf16[2,128,512]{2,1,0:T(8,128)(2,1)} %grad.1, f32[2,128,128]{2,1,0:T(8,128)} %bases_a.1, f32[2,128,128]{2,1,0:T(8,128)} %bases_g.1), custom_call_target="tpu_custom_call" | custom-call | flops 2000000000 | bytes 10000000 | tf_op jit(solution)/shard_map/pallas_call | solution.py:396
  44.8 1.7 %copy.8 = bf16[2,128,512]{2,1,0:T(8,128)(2,1)} copy(bf16[2,128,512]{2,1,0:T(8,128)(2,1)} %shard_map.64) | data formatting | bytes 524288

commit v3 on v1

v3 whole, which is shorter than its diff:
```python
import functools

import jax
import jax.numpy as jnp
from jax import lax
from jax.experimental import pallas as pl
from jax.experimental.pallas import tpu as pltpu
from jax.sharding import PartitionSpec as P

MESH = pl.DeviceIdType.MESH
B = 128
SLOTS = 2
DAMPING = 0.05
HIGHEST = lax.Precision.HIGHEST
F32 = jnp.float32

GROUP = 8 * B + 8
SET = 4 * B
ORDER = (2, 1, 3, 0)
SIDE = 16
FULL = 32500.0
TINY = 1e-37


def dot(a, b, ca, cb, precision=None):
    return lax.dot_general(a, b, (((ca,), (cb,)), ((), ())), precision=precision, preferred_element_type=F32)


def kernel(total_rows, slot_ref, acts, grads, grad, bases_a, bases_g, out,
           xs, gs, bs, part, core_in, own, code, norm, in_code, in_norm, in_two, in_row, row_sum, qc, qc_in, qs, qs_in, qm, qbuf, qa, qg,
           zs, zr, sa, sg, keep, rot, inner_s,
           ld, s_core, r_core, s_one, r_one, s_norm, r_norm, s_two, r_two, s_row, r_row, s_q, r_q, s_rs, r_rs, s_ag, r_ag,
           s_qy, r_qy, s_qx, r_qx, s_z, r_z, s_xy, r_xy, s_p, r_p):
    f = lax.axis_index("factor")
    d = lax.axis_index("dp")
    z_lo, c = f // 2, f % 2
    z_hi, y, x = d // 16, (d // 4) % 4, d % 4
    z = 4 * z_hi + z_lo
    other = 1 - c
    side = 1 - (y + c) % 2
    source_row = 2 * (z_lo % 2) + c
    is_source = y == source_row
    half_here = z_lo // 2

    def at(zz, yy, xx, cc):
        return (2 * (zz % 4) + cc, 16 * (zz // 4) + 4 * yy + xx)

    def column(k):
        return (y + (k + 1) // 4) % 4, (x + (k + 1) % 4) % 4

    def block(g, m):
        if m < 4:
            return 0, m, (x + ORDER[g]) % 4
        return 1, (y + ORDER[g]) % 4, m - 4

    def along(first, k):
        return at(z, y, (x + ORDER[k]) % 4, c) if first == 0 else at(z, (y + ORDER[k]) % 4, x, c)

    def remote(src, dst, send, recv, to):
        return pltpu.make_async_remote_copy(src_ref=src, dst_ref=dst, send_sem=send, recv_sem=recv,
                                            device_id=to, device_id_type=MESH)

    partner = at(z, y, x, other)
    barrier = pltpu.get_barrier_semaphore()

    def signal(to):
        pl.semaphore_signal(barrier, inc=1, device_id=to, device_id_type=MESH)

    signal(partner)
    for k in range(15):
        signal(at(z, *column(k), c))
    for k in range(1, 8):
        signal(at((z + k) % 8, y, x, c))

    load_a = pltpu.make_async_copy(bases_a, bs.at[0], ld.at[4])
    load_g = pltpu.make_async_copy(bases_g, bs.at[1], ld.at[5])
    load_grad = pltpu.make_async_copy(grad, gs, ld.at[6])

    def load_group(g):
        for m in range(8):
            h, yb, xb = block(g, m)
            cols = pl.ds(pl.multiple_of((16 * h + 4 * yb + xb) * B, B), B)
            for sd, tokens in ((0, acts), (1, grads)):
                pltpu.make_async_copy(tokens.at[:, :, cols], xs.at[g, m, sd], ld.at[g]).start()

    load_a.start()
    load_g.start()
    load_group(0)
    load_group(1)

    load_a.wait()
    load_g.wait()
    for l in range(2):
        slot = slot_ref[l]
        mine = (slot // SLOTS) == f
        for which, sd in ((0, side), (1, 1 - side)):
            picked = jnp.where(slot % SLOTS == 0, bs[sd, 0], bs[sd, 1])
            qc[which, l] = jnp.where(mine, picked, jnp.zeros_like(picked))
    norm[...] = jnp.zeros_like(norm)
    row_sum[...] = jnp.zeros_like(row_sum)
    pl.semaphore_wait(barrier, 23)

    core_q = remote(qc.at[1], qc_in, s_q, r_q, partner)
    core_q.start()
    load_group(2)
    load_group(3)
    load_grad.start()

    iota_r = lax.broadcasted_iota(jnp.int32, (B, B), 0)
    iota_c = lax.broadcasted_iota(jnp.int32, (B, B), 1)
    iota_16 = lax.broadcasted_iota(jnp.int32, (16, B), 0)
    upper = iota_r <= iota_c
    on_diag = iota_r == iota_c

    def norms_of(tile, row0, row1):
        right = tile.astype(jnp.bfloat16)

        def outer(row):
            return dot(jnp.where(iota_16 == row, tile, 0.0).astype(jnp.bfloat16), right, 0, 0)

        return jnp.where(upper, outer(row0), outer(row1))

    def terms(core, g, dst, add):
        for m in range(8):
            yb = block(g, m)[1]
            sd = 1 - (yb + core) % 2
            x0 = xs[g, m, sd, 0]
            x1 = xs[g, m, sd, 1]
            f0 = dot(x0, x0, 0, 0)
            f1 = dot(x1, x1, 0, 0)
            packed = jnp.where(upper, f0, f1)
            diag = jnp.sum(jnp.where(on_diag, f1, 0.0), axis=0, keepdims=True)
            rows = slice(m * B, (m + 1) * B)
            row = slice(8 * B + m, 8 * B + m + 1)
            if add is not None:
                packed = packed + add[rows, :]
                diag = diag + add[row, :]
            dst[rows, :] = packed
            dst[row, :] = diag

    core_copies, one_copies = [], []

    def for_partner(g):
        pltpu.make_async_copy(xs.at[g], xs.at[g], ld.at[g]).wait()
        terms(other, g, part.at[g], None)
        copy = remote(part.at[g], core_in.at[g], s_core.at[g], r_core.at[g], partner)
        copy.start()
        core_copies.append(copy)

    def for_plane(g):
        core_copies[g].wait_recv()
        terms(c, g, own.at[g], core_in.at[g])
        if g == 3:
            for w in range(2):
                row_sum[w, 0:4, :] = own[g, 8 * B + 4 * w : 8 * B + 4 * w + 4, :]
            return
        diag0 = [jnp.sum(jnp.where(on_diag, own[g, m * B : (m + 1) * B, :], 0.0), axis=0, keepdims=True)
                 for m in range(8)]
        diag1 = own[g, 8 * B :, :]
        diag = jnp.concatenate(diag0 + [diag1], axis=0)
        inverse = jnp.where(diag > TINY, lax.rsqrt(jnp.maximum(diag, TINY)), 1.0)
        tile = inverse.astype(jnp.bfloat16).astype(F32)
        for w in range(2):
            norm[w, g, 0:4, :] = tile[4 * w : 4 * w + 4, :]
            norm[w, g, 4:8, :] = tile[8 + 4 * w : 12 + 4 * w, :]
            norm[w, g, 8:12, :] = diag1[4 * w : 4 * w + 4, :]
            for i in range(4):
                m = 4 * w + i
                unit = own[g, m * B : (m + 1) * B, :] * norms_of(tile, m, 8 + m)
                code[w, g, i * B : (i + 1) * B, :] = jnp.round(unit * FULL).astype(jnp.int32).astype(jnp.int16)
            to = along(w, g)
            pair = (remote(norm.at[w, g], in_norm.at[w, g], s_norm.at[w, g], r_norm.at[w, g], to),
                    remote(code.at[w, g], in_code.at[w, g], s_one.at[w, g], r_one.at[w, g], to))
            for copy in pair:
                copy.start()
            one_copies.append(pair)

    def decode(w, g):
        for copy in one_copies[2 * g + w]:
            copy.wait_recv()
        tile = in_norm[w, g]
        for i in range(4):
            unit = in_code[w, g, i * B : (i + 1) * B, :].astype(jnp.int32).astype(F32) * (1.0 / FULL)
            own[3, (4 * w + i) * B : (4 * w + i + 1) * B, :] += unit / norms_of(tile, i, 4 + i)
        row_sum[w, 0:4, :] += in_norm[w, g, 8:12, :]

    two_copies = []

    def second(w):
        for k in range(3):
            to = along(1 - w, k)
            u = ((y, x)[w] + ORDER[k]) % 4
            rows = pl.ds(pl.multiple_of((4 * w + u) * B, B), B)
            for copy in (remote(row_sum.at[w], in_row.at[w, k], s_row.at[w, k], r_row.at[w, k], to),
                         remote(own.at[3, rows, :], in_two.at[w, k], s_two.at[w, k], r_two.at[w, k], to)):
                copy.start()
                two_copies.append(copy)

    for_partner(0)

    core_q.wait_recv()
    for l in range(2):
        qs[l] = qc[0, l] + qc_in[l]
    rs_copies = []
    for k in range(1, 4):
        zz = (z_lo + k) % 4
        copy = remote(qs.at[:, pl.ds(pl.multiple_of(32 * zz, 32), 32), :], qs_in.at[k - 1],
                      s_rs.at[k - 1], r_rs.at[k - 1], at(4 * z_hi + zz, y, x, c))
        copy.start()
        rs_copies.append(copy)

    for_partner(1)
    for_plane(0)
    for_partner(2)
    for_plane(1)
    for_partner(3)

    for copy in rs_copies:
        copy.wait_recv()
    here = pl.ds(pl.multiple_of(32 * z_lo, 32), 32)
    summed = qs[:, here, :] + qs_in[0] + qs_in[1] + qs_in[2]
    qm[...] = summed
    qbuf[z_hi, :, here, :] = summed
    ag_copies = []
    for k in range(1, 8):
        copy = remote(qm, qbuf.at[z_hi, :, here, :], s_ag.at[k - 1], r_ag.at[k - 1], at((z + k) % 8, y, x, c))
        copy.start()
        ag_copies.append(copy)

    for_plane(2)
    for_plane(3)
    for g in range(3):
        for w in range(2):
            decode(w, g)
            if g == 2:
                second(w)

    for k in range(1, 8):
        zz = (z + 8 - k) % 8
        rows = pl.ds(pl.multiple_of(32 * (zz % 4), 32), 32)
        remote(qm, qbuf.at[zz // 4, :, rows, :], s_ag.at[k - 1], r_ag.at[k - 1], partner).wait_recv()

    qy_copies = []
    for k in range(1, 4):
        copy = remote(qbuf.at[half_here], qg.at[x], s_qy.at[k - 1], r_qy, at(z, (y + k) % 4, x, c))
        qy_copies.append(copy)
    qa_copy = remote(qbuf.at[z_hi], qa, s_p.at[0], r_p.at[0], partner)

    @pl.when(is_source)
    def _():
        for copy in qy_copies:
            copy.start()
        qg[x] = qbuf[half_here]

    @pl.when(side == 0)
    def _():
        qa_copy.start()
        qa[...] = qbuf[z_hi]

    for copy in two_copies:
        copy.wait_recv()
    zs[...] = jnp.zeros_like(zs)
    for h in range(2):
        u = 4 * h + (y, x)[h]
        packed = own[3, pl.ds(pl.multiple_of(u * B, B), B), :] + in_two[h, 0] + in_two[h, 1] + in_two[h, 2]
        row = pl.ds((y, x)[h], 1)
        diag = row_sum[h, row, :] + in_row[h, 0, row, :] + in_row[h, 1, row, :] + in_row[h, 2, row, :]
        m0 = jnp.where(upper, jnp.where(on_diag, packed, 2.0 * packed), 0.0)
        m1 = jnp.where(upper, jnp.where(on_diag, jnp.broadcast_to(diag, (B, B)), 0.0), 2.0 * packed)
        for l, m in ((0, m0), (1, m1)):
            q = qbuf[h, l]
            zs[2 * h + l : 2 * h + l + 1, :] = jnp.sum(q * dot(m, q, 1, 0, HIGHEST), axis=0, keepdims=True)
    z_copies = []
    for k in range(1, 8):
        copy = remote(zs, zr.at[k], s_z.at[k - 1], r_z.at[k - 1], at((z + k) % 8, y, x, c))
        copy.start()
        z_copies.append(copy)
    zr[0] = zs[...]

    @pl.when(jnp.logical_not(is_source))
    def _():
        qy_copies[0].wait_recv()

    qx_copies = []
    for k in range(1, 4):
        copy = remote(qg.at[x], qg.at[x], s_qx.at[k - 1], r_qx.at[k - 1], at(z, y, (x + k) % 4, c))
        copy.start()
        qx_copies.append(copy)

    @pl.when(side == 1)
    def _():
        qa_copy.wait_recv()

    load_grad.wait()
    for l in range(2):
        rot[l] = dot(qa[l], gs[l].astype(F32), 0, 0, HIGHEST)

    for copy in z_copies:
        copy.wait_recv()
    scales = zr[0]
    for k in range(1, 8):
        scales = scales + zr[k]
    scales = scales / total_rows
    keep[...] = scales

    xy_copies = []
    for k in range(15):
        xy_copies.append(remote(zs, sg.at[x], s_xy.at[k], r_xy.at[x], at(z, *column(k), c)))
    sa_copy = remote(zs, sa, s_p.at[1], r_p.at[1], partner)

    for copy in z_copies:
        copy.wait_send()

    @pl.when(is_source)
    def _():
        zs[:2, :] = keep[pl.ds(2 * half_here, 2), :]
        for copy in xy_copies:
            copy.start()
        sg[x] = zs[...]

    @pl.when(side == 0)
    def _():
        zs[:2, :] = keep[pl.ds(2 * z_hi, 2), :]
        sa_copy.start()
        sa[...] = zs[...]

    @pl.when(side == 1)
    def _():
        sa_copy.wait_recv()

    def turn(q):
        cols = pl.ds(pl.multiple_of(q * B, B), B)
        for l in range(2):
            inner_s[l, :, cols] = dot(rot[l, :, cols], qg[q, l], 1, 0, HIGHEST)

    turn(x)
    for k in (1, 3, 2):
        from_x = (x + 4 - k) % 4
        remote(qg.at[x], qg.at[from_x], s_qx.at[k - 1], r_qx.at[k - 1], partner).wait_recv()
        turn(from_x)

    for q in range(4):
        @pl.when(jnp.logical_not(jnp.logical_and(is_source, x == q)))
        def _():
            remote(zs, sg.at[q], s_xy.at[0], r_xy.at[q], partner).wait_recv()

    for l in range(2):
        left = jnp.transpose(jnp.broadcast_to(sa[l : l + 1, :], (B, B)))
        for q in range(4):
            cols = slice(q * B, (q + 1) * B)
            scaled = inner_s[l, :, cols] / (left * sg[q, l : l + 1, :] + DAMPING)
            inner_s[l, :, cols] = dot(scaled, qg[q, l], 1, 1, HIGHEST)
        out[l] = dot(qa[l], inner_s[l], 1, 0, HIGHEST).astype(out.dtype)

    for pair in one_copies:
        for copy in pair:
            copy.wait_send()
    for copy in [core_q] + core_copies + two_copies + rs_copies + ag_copies + qx_copies:
        copy.wait_send()

    @pl.when(is_source)
    def _():
        for copy in qy_copies + xy_copies:
            copy.wait_send()

    @pl.when(side == 0)
    def _():
        qa_copy.wait_send()
        sa_copy.wait_send()


def body(acts, grads_out, grad, bases_a, bases_g, owner_slot):
    rows = acts.shape[1]
    total_rows = rows * lax.axis_size("dp") * lax.axis_size("factor")
    dma = pltpu.SemaphoreType.DMA
    scratch = [
        pltpu.VMEM((4, 8, 2, 2, rows, B), acts.dtype),
        pltpu.VMEM(grad.shape, grad.dtype),
        pltpu.VMEM((2,) + bases_a.shape, F32),
        pltpu.VMEM((4, GROUP, B), F32),
        pltpu.VMEM((4, GROUP, B), F32),
        pltpu.VMEM((4, GROUP, B), F32),
        pltpu.VMEM((2, 3, SET, B), jnp.int16),
        pltpu.VMEM((2, 3, SIDE, B), F32),
        pltpu.VMEM((2, 3, SET, B), jnp.int16),
        pltpu.VMEM((2, 3, SIDE, B), F32),
        pltpu.VMEM((2, 3, B, B), F32),
        pltpu.VMEM((2, 3, 8, B), F32),
        pltpu.VMEM((2, 8, B), F32),
        pltpu.VMEM((2, 2, B, B), F32),
        pltpu.VMEM((2, B, B), F32),
        pltpu.VMEM((2, B, B), F32),
        pltpu.VMEM((3, 2, 32, B), F32),
        pltpu.VMEM((2, 32, B), F32),
        pltpu.VMEM((2, 2, B, B), F32),
        pltpu.VMEM((2, B, B), F32),
        pltpu.VMEM((4, 2, B, B), F32),
        pltpu.VMEM((8, B), F32),
        pltpu.VMEM((8, 8, B), F32),
        pltpu.VMEM((8, B), F32),
        pltpu.VMEM((4, 8, B), F32),
        pltpu.VMEM((8, B), F32),
        pltpu.VMEM((2, B, 4 * B), F32),
        pltpu.VMEM((2, B, 4 * B), F32),
        dma((7,)),
        dma((4,)), dma((4,)),
        dma((2, 3)), dma((2, 3)),
        dma((2, 3)), dma((2, 3)),
        dma((2, 3)), dma((2, 3)),
        dma((2, 3)), dma((2, 3)),
        dma, dma,
        dma((3,)), dma((3,)),
        dma((7,)), dma((7,)),
        dma((3,)), dma,
        dma((3,)), dma((3,)),
        dma((7,)), dma((7,)),
        dma((15,)), dma((4,)),
        dma((2,)), dma((2,)),
    ]
    hbm = pl.BlockSpec(memory_space=pltpu.HBM)
    return pl.pallas_call(
        functools.partial(kernel, total_rows),
        out_shape=jax.ShapeDtypeStruct(grad.shape, jnp.bfloat16),
        in_specs=[pl.BlockSpec(memory_space=pltpu.SMEM)] + [hbm] * 5,
        out_specs=pl.BlockSpec(memory_space=pltpu.VMEM),
        scratch_shapes=scratch,
        compiler_params=pltpu.CompilerParams(
            collective_id=0, has_side_effects=True, vmem_limit_bytes=63 * 1024 * 1024
        ),
        cost_estimate=pl.CostEstimate(flops=2 * 10**9, bytes_accessed=10**7, transcendentals=0),
    )(owner_slot, acts, grads_out, grad, bases_a, bases_g)


def solution(mesh):
    tokens = P(None, ("factor", "dp"), None)
    bases = P("factor", "dp", None)
    split = P(None, "dp", "factor")
    in_specs = (tokens, tokens, split, bases, bases, P())
    return jax.shard_map(body, mesh=mesh, in_specs=in_specs, out_specs=split, check_vma=False)
```

time: 59.6 us -> 44.2 us (0.74)
  the two profiles are of different devices: /device:TPU:33 before, /device:TPU:32 now
where the time goes in v3:
time: 44.2 us; the launch traced here: 44 us
  Pallas kernels  42.4 us (96%)
  local copies, waits for them, and re-layouts  1.67 us (4%)
    pallas_call x1, Pallas kernels, body(): pl.pallas_call(functools.partial(kernel, total_rows), out_shape=jax.Shape...  42.4 us
    unnamed x1, local copies, waits for them, and re-layouts  1.67 us

profile of v3, /device:TPU:32, one launch (start us, length us, event | category | flops | bytes accessed | tf_op | source)
XLA Modules:
  0.0 44.0 jit_solution(11174531496840653654)
XLA Ops:
  0.0 42.4 %shard_map.64 = bf16[2,128,512]{2,1,0:T(8,128)(2,1)} custom-call(s32[2]{0:T(128)} %slot_ref.1, bf16[2,256,4096]{2,1,0:T(8,128)(2,1)} %acts.1, bf16[2,256,4096]{2,1,0:T(8,128)(2,1)} %grads.1, bf16[2,128,512]{2,1,0:T(8,128)(2,1)} %grad.1, f32[2,128,128]{2,1,0:T(8,128)} %bases_a.1, f32[2,128,128]{2,1,0:T(8,128)} %bases_g.1), custom_call_target="tpu_custom_call" | custom-call | flops 2000000000 | bytes 10000000 | tf_op jit(solution)/shard_map/pallas_call | solution.py:421
  42.4 1.7 %copy.8 = bf16[2,128,512]{2,1,0:T(8,128)(2,1)} copy(bf16[2,128,512]{2,1,0:T(8,128)(2,1)} %shard_map.64) | data formatting | bytes 524288

commit v4 on v3

--- a/solution.py
+++ b/solution.py
@@ -11,7 +11,6 @@
 B = 128
 SLOTS = 2
 DAMPING = 0.05
-HIGHEST = lax.Precision.HIGHEST
 F32 = jnp.float32
 
 GROUP = 8 * B + 8
@@ -24,6 +23,16 @@
 
 def dot(a, b, ca, cb, precision=None):
     return lax.dot_general(a, b, (((ca,), (cb,)), ((), ())), precision=precision, preferred_element_type=F32)
+
+
+def halves(a):
+    high = a.astype(jnp.bfloat16)
+    return high, (a - high.astype(F32)).astype(jnp.bfloat16)
+
+
+def dot3(a, b, ca, cb):
+    (ah, al), (bh, bl) = halves(a), halves(b)
+    return dot(ah, bh, ca, cb) + (dot(ah, bl, ca, cb) + dot(al, bh, ca, cb))
 
 
 def kernel(total_rows, slot_ref, acts, grads, grad, bases_a, bases_g, out,
@@ -215,6 +224,8 @@
     for_plane(1)
     for_partner(3)
 
+    for_plane(2)
+
     for copy in rs_copies:
         copy.wait_recv()
     here = pl.ds(pl.multiple_of(32 * z_lo, 32), 32)
@@ -227,7 +238,6 @@
         copy.start()
         ag_copies.append(copy)
 
-    for_plane(2)
     for_plane(3)
     for g in range(3):
         for w in range(2):
@@ -269,7 +279,7 @@
         m1 = jnp.where(upper, jnp.where(on_diag, jnp.broadcast_to(diag, (B, B)), 0.0), 2.0 * packed)
         for l, m in ((0, m0), (1, m1)):
             q = qbuf[h, l]
-            zs[2 * h + l : 2 * h + l + 1, :] = jnp.sum(q * dot(m, q, 1, 0, HIGHEST), axis=0, keepdims=True)
+            zs[2 * h + l : 2 * h + l + 1, :] = jnp.sum(q * dot3(m, q, 1, 0), axis=0, keepdims=True)
     z_copies = []
     for k in range(1, 8):
         copy = remote(zs, zr.at[k], s_z.at[k - 1], r_z.at[k - 1], at((z + k) % 8, y, x, c))
@@ -293,7 +303,8 @@
 
     load_grad.wait()
     for l in range(2):
-        rot[l] = dot(qa[l], gs[l].astype(F32), 0, 0, HIGHEST)
+        high, low = halves(qa[l])
+        rot[l] = dot(high, gs[l], 0, 0) + dot(low, gs[l], 0, 0)
 
     for copy in z_copies:
         copy.wait_recv()
@@ -331,7 +342,7 @@
     def turn(q):
         cols = pl.ds(pl.multiple_of(q * B, B), B)
         for l in range(2):
-            inner_s[l, :, cols] = dot(rot[l, :, cols], qg[q, l], 1, 0, HIGHEST)
+            inner_s[l, :, cols] = dot3(rot[l, :, cols], qg[q, l], 1, 0)
 
     turn(x)
     for k in (1, 3, 2):
@@ -349,8 +360,8 @@
         for q in range(4):
             cols = slice(q * B, (q + 1) * B)
             scaled = inner_s[l, :, cols] / (left * sg[q, l : l + 1, :] + DAMPING)
-            inner_s[l, :, cols] = dot(scaled, qg[q, l], 1, 1, HIGHEST)
-        out[l] = dot(qa[l], inner_s[l], 1, 0, HIGHEST).astype(out.dtype)
+            inner_s[l, :, cols] = dot3(scaled, qg[q, l], 1, 1)
+        out[l] = dot3(qa[l], inner_s[l], 1, 0).astype(out.dtype)
 
     for pair in one_copies:
         for copy in pair:

time: 44.2 us -> 43.1 us (0.975)
  Pallas kernels: 42.4 us -> 41.3 us
    pallas_call x1, Pallas kernels: 42.4 us -> 41.3 us  [body(): pl.pallas_call(functools.partial(kernel, total_rows), out_shape=jax.Shape...]
where the time goes in v4:
time: 43.1 us; the launch traced here: 43 us
  Pallas kernels  41.3 us (96%)
  local copies, waits for them, and re-layouts  1.67 us (4%)
    pallas_call x1, Pallas kernels, body(): pl.pallas_call(functools.partial(kernel, total_rows), out_shape=jax.Shape...  41.3 us
    unnamed x1, local copies, waits for them, and re-layouts  1.67 us

profile of v4, /device:TPU:32, one launch (start us, length us, event | category | flops | bytes accessed | tf_op | source)
XLA Modules:
  0.0 43.0 jit_solution(12417744451623986612)
XLA Ops:
  0.0 41.3 %shard_map.64 = bf16[2,128,512]{2,1,0:T(8,128)(2,1)} custom-call(s32[2]{0:T(128)} %slot_ref.1, bf16[2,256,4096]{2,1,0:T(8,128)(2,1)} %acts.1, bf16[2,256,4096]{2,1,0:T(8,128)(2,1)} %grads.1, bf16[2,128,512]{2,1,0:T(8,128)(2,1)} %grad.1, f32[2,128,128]{2,1,0:T(8,128)} %bases_a.1, f32[2,128,128]{2,1,0:T(8,128)} %bases_g.1), custom_call_target="tpu_custom_call" | custom-call | flops 2000000000 | bytes 10000000 | tf_op jit(solution)/shard_map/pallas_call | solution.py:432
  41.3 1.7 %copy.8 = bf16[2,128,512]{2,1,0:T(8,128)(2,1)} copy(bf16[2,128,512]{2,1,0:T(8,128)(2,1)} %shard_map.64) | data formatting | bytes 524288

commit v5 on v4

--- a/solution.py
+++ b/solution.py
@@ -75,12 +75,6 @@
     def signal(to):
         pl.semaphore_signal(barrier, inc=1, device_id=to, device_id_type=MESH)
 
-    signal(partner)
-    for k in range(15):
-        signal(at(z, *column(k), c))
-    for k in range(1, 8):
-        signal(at((z + k) % 8, y, x, c))
-
     load_a = pltpu.make_async_copy(bases_a, bs.at[0], ld.at[4])
     load_g = pltpu.make_async_copy(bases_g, bs.at[1], ld.at[5])
     load_grad = pltpu.make_async_copy(grad, gs, ld.at[6])
@@ -95,6 +89,13 @@
     load_a.start()
     load_g.start()
     load_group(0)
+
+    signal(partner)
+    for k in range(15):
+        signal(at(z, *column(k), c))
+    for k in range(1, 8):
+        signal(at((z + k) % 8, y, x, c))
+
     load_group(1)
 
     load_a.wait()

time: 43.1 us -> 43.1 us (level)
  no operation moved by 1% of the time
where the time goes in v5:
time: 43.1 us; the launch traced here: 43 us
  Pallas kernels  41.3 us (96%)
  local copies, waits for them, and re-layouts  1.67 us (4%)
    pallas_call x1, Pallas kernels, body(): pl.pallas_call(functools.partial(kernel, total_rows), out_shape=jax.Shape...  41.3 us
    unnamed x1, local copies, waits for them, and re-layouts  1.67 us

profile of v5, /device:TPU:32, one launch (start us, length us, event | category | flops | bytes accessed | tf_op | source)
XLA Modules:
  0.0 43.0 jit_solution(11360233803831132688)
XLA Ops:
  0.0 41.3 %shard_map.64 = bf16[2,128,512]{2,1,0:T(8,128)(2,1)} custom-call(s32[2]{0:T(128)} %slot_ref.1, bf16[2,256,4096]{2,1,0:T(8,128)(2,1)} %acts.1, bf16[2,256,4096]{2,1,0:T(8,128)(2,1)} %grads.1, bf16[2,128,512]{2,1,0:T(8,128)(2,1)} %grad.1, f32[2,128,128]{2,1,0:T(8,128)} %bases_a.1, f32[2,128,128]{2,1,0:T(8,128)} %bases_g.1), custom_call_target="tpu_custom_call" | custom-call | flops 2000000000 | bytes 10000000 | tf_op jit(solution)/shard_map/pallas_call | solution.py:433
  41.3 1.7 %copy.8 = bf16[2,128,512]{2,1,0:T(8,128)(2,1)} copy(bf16[2,128,512]{2,1,0:T(8,128)(2,1)} %shard_map.64) | data formatting | bytes 524288
